TPU v7x, 512 devices: a whole 4x8x8 slice. The times are simulated.
512 devices in a mesh: gx: 32 (over x, z), gy: 16 (over y, core).
Axes of the slice: x: 4, y: 8, z: 8, core: 2. Of those that a mesh axis runs over, the one named last changes fastest.
Arguments:
- forcing_terms: float32 [32, 16, 64, 512], P('gx', 'gy'), may hold values from -6 to 6
- schur: bfloat16 [32, 16, 1024, 1024], P('gx', 'gy'), as said below
- flexibility: bfloat16 [32, 16, 1024, 1024], P('gx', 'gy'), as said below
- coarse_modes: float32 [32, 16, 8, 512], P('gx', 'gy'), may hold values from -1.2 to 1.2
- coarse_map: int32 [32, 16, 8], P('gx', 'gy'), may hold values from 0 to 511, as said below
- face_slot_count: int32 [32, 16, 2], P('gx', 'gy'), may hold values from 128 to 256, as said below
- coarse_inverse: bfloat16 [512, 512], replicated, as said below
Outputs:
- multipliers: float32 [32, 16, 64, 512], P('gx', 'gy')
- residual: float32 [32, 16, 64, 512], P('gx', 'gy')
Inputs may be any that keep to these rules, and one draw needn't show every extreme that they name: coarse_map[s, c, k] = min(s + a, 31) * 16 + min(c + b, 15) with a and b each 0 or 1, both 0 for k = 0. `face_slot_count`: some face in every draw has exactly 256 live slots. `schur`: symmetric positive definite. `flexibility`: symmetric positive definite. `coarse_inverse`: symmetric positive definite.
All inputs are finite; a program needn't handle non-finite values.
Results may differ from a plain program's by a relative error of at most 0.0043.
Values may be sent and summed in bfloat16 or wider, within the bound.
A program may use at most 64 MiB of HBM per device.

v0:
```python
import jax
import jax.numpy as jnp
from jax import lax
from jax.sharding import PartitionSpec as P

ITERS = 2


highest = lax.Precision.HIGHEST


def passed_along(block, axis, distance):
    devices = range(lax.axis_size(axis))
    route = [(i - distance, i) for i in devices if i - distance in devices]
    return lax.ppermute(block, axis, route)


def distribute_values(multiplier_vector, slot_width):
    halves = multiplier_vector.astype(jnp.bfloat16)
    own_x = halves[:, :slot_width]
    own_y = halves[:, slot_width:]
    below_x = passed_along(own_x, "gx", 1)
    below_y = passed_along(own_y, "gy", 1)
    return jnp.concatenate([-below_x, own_x, -below_y, own_y], axis=1)


def gather_owned(operator_images, slot_activity, slot_width):
    upper_neighbour_x = passed_along(operator_images[:, :slot_width], "gx", -1)
    upper_neighbour_y = passed_along(operator_images[:, 2 * slot_width : 3 * slot_width], "gy", -1)
    combined_parts = jnp.concatenate(
        [
            operator_images[:, slot_width : 2 * slot_width] - upper_neighbour_x,
            operator_images[:, 3 * slot_width :] - upper_neighbour_y,
        ],
        axis=1,
    )
    return slot_activity * combined_parts


def corner_terms(multiplier_vector, filtered_modes, selector):
    local_terms = jnp.dot(multiplier_vector, filtered_modes.T, precision=highest)
    return jnp.dot(local_terms, selector, precision=highest)


def assemble_corners(scattered):
    return lax.psum(scattered, ("gx", "gy"))


def coarse_from_sums(corner_sums, filtered_modes, selector, coarse_inverse):
    solved = jnp.dot(
        corner_sums.astype(jnp.bfloat16), coarse_inverse, preferred_element_type=jnp.float32
    )
    picked = jnp.dot(solved, selector.T, precision=highest)
    return jnp.dot(picked, filtered_modes, precision=highest)


def residual_sum(residual, smoothed):
    return lax.psum(jnp.sum(residual * smoothed, axis=1), ("gx", "gy"))


def on_device(
    forcing_terms, schur, flexibility, coarse_modes, coarse_map, face_slot_count, coarse_inverse
):
    slot_width = forcing_terms.shape[3] // 2
    sides = forcing_terms.shape[2]
    slab_index = lax.axis_index("gx")
    column_index = lax.axis_index("gy")
    slab_count = lax.axis_size("gx")
    column_count = lax.axis_size("gy")
    lengths = face_slot_count[0, 0]
    positions = jnp.arange(slot_width, dtype=jnp.int32)
    active_slots_x = jnp.logical_and(positions < lengths[0], slab_index < slab_count - 1)
    active_slots_y = jnp.logical_and(positions < lengths[1], column_index < column_count - 1)
    slot_activity = jnp.concatenate([active_slots_x, active_slots_y]).astype(jnp.float32)[None, :]
    stiffness = schur[0, 0]
    compliance = flexibility[0, 0]
    filtered_modes = coarse_modes[0, 0] * slot_activity
    coarse_count = coarse_inverse.shape[0]
    selector = (
        coarse_map[0, 0][:, None] == jnp.arange(coarse_count, dtype=jnp.int32)[None, :]
    ).astype(jnp.float32)

    def finish(multiplier_vector, corner_sums):
        operator_images = jnp.dot(
            distribute_values(multiplier_vector, slot_width),
            stiffness,
            preferred_element_type=jnp.float32,
        )
        dirichlet_part = 0.25 * gather_owned(operator_images, slot_activity, slot_width)
        return dirichlet_part + coarse_from_sums(
            corner_sums, filtered_modes, selector, coarse_inverse
        )

    def precondition(multiplier_vector):
        corner_sums = assemble_corners(corner_terms(multiplier_vector, filtered_modes, selector))
        return finish(multiplier_vector, corner_sums)

    residual = slot_activity * forcing_terms[0, 0]
    multipliers = jnp.zeros_like(residual)
    search = precondition(residual)
    product = residual_sum(residual, search)
    for iteration in range(ITERS):
        operator_operator_images = jnp.dot(
            distribute_values(search, slot_width), compliance, preferred_element_type=jnp.float32
        )
        fresh_image = gather_owned(operator_operator_images, slot_activity, slot_width)
        curvature = lax.psum(jnp.sum(search * fresh_image, axis=1), ("gx", "gy"))
        step_size = product / curvature
        multipliers = multipliers + step_size[:, None] * search
        residual = residual - step_size[:, None] * fresh_image
        if iteration + 1 < ITERS:
            smoothed = precondition(residual)
            product_next = residual_sum(residual, smoothed)
            search = smoothed + (product_next / product)[:, None] * search
            product = product_next
    return (
        multipliers.reshape(1, 1, sides, 2 * slot_width),
        residual.reshape(1, 1, sides, 2 * slot_width),
    )


def solution(mesh):
    return jax.shard_map(
        on_device,
        mesh=mesh,
        in_specs=(
            P("gx", "gy", None, None),
            P("gx", "gy", None, None),
            P("gx", "gy", None, None),
            P("gx", "gy", None, None),
            P("gx", "gy", None),
            P("gx", "gy", None),
            P(),
        ),
        out_specs=(P("gx", "gy", None, None), P("gx", "gy", None, None)),
        check_vma=False,
    )
```

profile of v0, /device:TPU:1, one launch (start us, length us, event | category | flops | bytes accessed | tf_op | source)
XLA Modules:
  0.0 586.0 jit_solution(17941656161500811876)
XLA Ops:
  0.6 0.0 copy-start
  0.7 1.4 fusion.86
  2.1 1.3 compare_and_fusion
  3.4 0.9 fusion.51
  4.3 4.8 collective-permute-start
  9.2 4.0 collective-permute-start.1
  13.2 1.2 fusion.48
  14.4 0.0 copy-start.5
  14.4 1.0 fusion.62
  15.4 102.4 %all-reduce.3 = bf16[64,512]{1,0:T(8,128)(2,1)S(1)} all-reduce(f32[64,512]{1,0:T(8,128)S(1)} %fusion.62), channel_id=1, replica_groups=mesh['gx'=32,'gy'=16] {'gx','gy'}, use_global_device_ids=true, to_apply=%region_0.0 | all-reduce | flops 32768 | bytes 196608 | tf_op jit(solution)/shard_map/psum | solution.py:46
  117.8 0.0 copy-start.4
  117.8 0.0 collective-permute-done
  117.8 0.0 collective-permute-done.1
  117.8 0.0 copy-start.1
  117.9 0.5 fusion.6
  118.4 1.4 collective-permute-start.2
  119.8 0.2 fusion.89
  120.0 3.5 collective-permute-done.2
  123.5 0.0 copy-start.2
  123.5 3.9 collective-permute-start.3
  127.4 0.3 fusion.61
  127.7 3.2 collective-permute-done.3
  130.9 0.2 fusion.87
  131.1 1.3 collective-permute-start.4
  132.4 2.1 collective-permute-start.5
  134.6 0.0 collective-permute-done.4
  134.6 1.0 collective-permute-done.5
  135.6 0.5 fusion.2
  136.1 1.3 collective-permute-start.6
  137.4 4.3 collective-permute-done.6
  141.7 2.8 collective-permute-start.7
  144.5 4.2 collective-permute-done.7
  148.7 0.1 multiply_reduce_fusion.1
  148.9 100.4 %all-reduce = (f32[64]{0:T(128)S(1)}, f32[64]{0:T(128)S(1)}) all-reduce(f32[64]{0:T(128)S(1)} %get-tuple-element.3, f32[64]{0:T(128)S(1)} %get-tuple-element.2), channel_id=1, replica_groups=mesh['gx'=32,'gy'=16] {'gx','gy'}, use_global_device_ids=true, to_apply=%region_2.0 | all-reduce | flops 128 | bytes 1024 | tf_op jit(solution)/shard_map/psum | solution.py:58
  249.2 0.1 fusion.80
  249.3 1.3 collective-permute-start.8
  250.6 4.9 collective-permute-start.9
  255.5 0.3 fusion.46
  255.8 0.2 fusion.60
  256.1 97.5 %all-reduce.4 = bf16[64,512]{1,0:T(8,128)(2,1)S(1)} all-reduce(f32[64,512]{1,0:T(8,128)S(1)} %fusion.60), channel_id=1, replica_groups=mesh['gx'=32,'gy'=16] {'gx','gy'}, use_global_device_ids=true, to_apply=%region_5.0 | all-reduce | flops 32768 | bytes 196608 | tf_op jit(solution)/shard_map/psum | solution.py:46
  353.6 0.0 collective-permute-done.9
  353.6 0.5 fusion.4
  354.1 1.3 collective-permute-start.10
  355.4 0.2 fusion.88
  355.7 3.5 collective-permute-done.10
  359.2 3.8 collective-permute-start.11
  362.9 0.3 fusion.59
  363.2 1.6 collective-permute-done.11
  364.8 0.4 multiply_reduce_fusion
  365.1 97.4 %psum.46 = f32[64]{0:T(128)S(1)} all-reduce(f32[64]{0:T(128)S(1)} %get-tuple-element.28), channel_id=1, replica_groups=mesh['gx'=32,'gy'=16] {'gx','gy'}, use_global_device_ids=true, to_apply=%region_7.0 | all-reduce | flops 64 | bytes 512 | tf_op jit(solution)/shard_map/psum | solution.py:58
  462.5 0.1 fusion.81
  462.6 2.3 collective-permute-start.12
  464.9 4.0 collective-permute-start.13
  468.9 0.0 collective-permute-done.12
  469.0 1.0 collective-permute-done.13
  470.0 2.1 fusion
  472.0 1.3 collective-permute-start.14
  473.3 3.7 collective-permute-done.14
  477.1 1.9 collective-permute-start.15
  479.0 5.4 collective-permute-done.15
  484.4 0.1 fusion.43
  484.5 99.9 %psum.47 = f32[64]{0:T(128)S(1)} all-reduce(f32[64]{0:T(128)S(1)} %fusion.43), channel_id=1, replica_groups=mesh['gx'=32,'gy'=16] {'gx','gy'}, use_global_device_ids=true, to_apply=%region_9.0 | all-reduce | flops 64 | bytes 512 | tf_op jit(solution)/shard_map/psum | solution.py:107
  584.5 0.7 add_bitcast_fusion
  585.2 0.7 fusion.45
  (36 shorter events, 0.3 us)
Async XLA Ops:
  0.6 117.2 %copy-start = (bf16[1,1,1024,1024]{3,2,1,0:T(8,128)(2,1)S(1)}, bf16[1,1,1024,1024]{3,2,1,0:T(8,128)(2,1)}, u32[]{:S(2)}) copy-start(bf16[1,1,1024,1024]{3,2,1,0:T(8,128)(2,1)} %param.8) | copy-start | bytes 6291460
  0.6 119.1 %copy-start.3 = (bf16[512,512]{1,0:T(8,128)(2,1)S(1)}, bf16[512,512]{1,0:T(8,128)(2,1)}, u32[]{:S(2)}) copy-start(bf16[512,512]{1,0:T(8,128)(2,1)} %param.13) | copy-start | bytes 1572868
  4.3 113.5 %collective-permute-start = (bf16[64,256]{1,0:T(8,128)(2,1)S(1)}, bf16[64,256]{1,0:T(8,128)(2,1)S(1)}, u32[]{:S(2)}, u32[]{:S(2)}) collective-permute-start(bf16[64,256]{1,0:T(8,128)(2,1)S(1)} %get-tuple-element.22), channel_id=1, source_target_pairs={{0,16},{16,32},{32,48},{48,64},{64,80},{80,96},{96,112},{112,128},... | collective-permute-start | bytes 98312 | tf_op jit(solution)/shard_map/ppermute | solution.py:15
  9.2 108.7 %collective-permute-start.1 = (bf16[64,256]{1,0:T(8,128)(2,1)S(1)}, bf16[64,256]{1,0:T(8,128)(2,1)S(1)}, u32[]{:S(2)}, u32[]{:S(2)}) collective-permute-start(bf16[64,256]{1,0:T(8,128)(2,1)S(1)} %get-tuple-element.23), channel_id=1, source_target_pairs={{0,1},{1,2},{2,3},{3,4},{4,5},{5,6},{6,7},{7,8},{8,9},{9,10},{10,1... | collective-permute-start | bytes 98312 | tf_op jit(solution)/shard_map/ppermute | solution.py:15
  14.4 113.0 %copy-start.5 = (s32[1,1,8]{2,1,0:T(1,128)S(1)}, s32[1,1,8]{2,1,0:T(1,128)}, u32[]{:S(2)}) copy-start(s32[1,1,8]{2,1,0:T(1,128)} %param.11) | copy-start | bytes 100
  117.8 13.1 %copy-start.4 = (f32[1,1,8,512]{3,2,1,0:T(8,128)S(1)}, f32[1,1,8,512]{3,2,1,0:T(8,128)}, u32[]{:S(2)}) copy-start(f32[1,1,8,512]{3,2,1,0:T(8,128)} %param.10) | copy-start | bytes 49156
  117.8 17.8 %copy-start.1 = (bf16[1,1,1024,1024]{3,2,1,0:T(8,128)(2,1)S(1)}, bf16[1,1,1024,1024]{3,2,1,0:T(8,128)(2,1)}, u32[]{:S(2)}) copy-start(bf16[1,1,1024,1024]{3,2,1,0:T(8,128)(2,1)} %param.9) | copy-start | bytes 6291460
  118.4 5.1 collective-permute-start.2
  123.5 25.2 %copy-start.2 = (f32[1,1,64,512]{3,2,1,0:T(8,128)S(1)}, f32[1,1,64,512]{3,2,1,0:T(8,128)}, u32[]{:S(2)}) copy-start(f32[1,1,64,512]{3,2,1,0:T(8,128)} %param.7) | copy-start | bytes 393220
  123.5 7.3 %collective-permute-start.3 = (f32[64,256]{1,0:T(8,128)S(1)}, f32[64,256]{1,0:T(8,128)S(1)}, u32[]{:S(2)}, u32[]{:S(2)}) collective-permute-start(f32[64,256]{1,0:T(8,128)S(1)} %get-tuple-element.15), channel_id=1, source_target_pairs={{1,0},{2,1},{3,2},{4,3},{5,4},{6,5},{7,6},{8,7},{9,8},{10,9},{11,1... | collective-permute-start | bytes 196616 | tf_op jit(solution)/shard_map/ppermute | solution.py:15
  131.1 3.5 collective-permute-start.4
  132.4 3.2 collective-permute-start.5
  136.1 5.6 collective-permute-start.6
  141.7 7.0 %collective-permute-start.7 = (f32[64,256]{1,0:T(8,128)S(1)}, f32[64,256]{1,0:T(8,128)S(1)}, u32[]{:S(2)}, u32[]{:S(2)}) collective-permute-start(f32[64,256]{1,0:T(8,128)S(1)} %get-tuple-element.13), channel_id=1, source_target_pairs={{1,0},{2,1},{3,2},{4,3},{5,4},{6,5},{7,6},{8,7},{9,8},{10,9},{11,1... | collective-permute-start | bytes 196616 | tf_op jit(solution)/shard_map/ppermute | solution.py:15
  249.3 104.2 %collective-permute-start.8 = (bf16[64,256]{1,0:T(8,128)(2,1)S(1)}, bf16[64,256]{1,0:T(8,128)(2,1)S(1)}, u32[]{:S(2)}, u32[]{:S(2)}) collective-permute-start(bf16[64,256]{1,0:T(8,128)(2,1)S(1)} %get-tuple-element.18), channel_id=1, source_target_pairs={{0,16},{16,32},{32,48},{48,64},{64,80},{80,96},{96,112},{112,128},... | collective-permute-start | bytes 98312 | tf_op jit(solution)/shard_map/ppermute | solution.py:15
  250.6 103.0 %collective-permute-start.9 = (bf16[64,256]{1,0:T(8,128)(2,1)S(1)}, bf16[64,256]{1,0:T(8,128)(2,1)S(1)}, u32[]{:S(2)}, u32[]{:S(2)}) collective-permute-start(bf16[64,256]{1,0:T(8,128)(2,1)S(1)} %get-tuple-element.19), channel_id=1, source_target_pairs={{0,1},{1,2},{2,3},{3,4},{4,5},{5,6},{6,7},{7,8},{8,9},{9,10},{10,1... | collective-permute-start | bytes 98312 | tf_op jit(solution)/shard_map/ppermute | solution.py:15
  354.1 5.0 collective-permute-start.10
  359.2 5.6 collective-permute-start.11
  462.6 6.3 %collective-permute-start.12 = (bf16[64,256]{1,0:T(8,128)(2,1)S(1)}, bf16[64,256]{1,0:T(8,128)(2,1)S(1)}, u32[]{:S(2)}, u32[]{:S(2)}) collective-permute-start(bf16[64,256]{1,0:T(8,128)(2,1)S(1)} %get-tuple-element.16), channel_id=1, source_target_pairs={{0,16},{16,32},{32,48},{48,64},{64,80},{80,96},{96,112},{112,128},... | collective-permute-start | bytes 98312 | tf_op jit(solution)/shard_map/ppermute | solution.py:15
  464.9 5.1 collective-permute-start.13
  472.0 5.0 collective-permute-start.14
  477.1 7.3 %collective-permute-start.15 = (f32[64,256]{1,0:T(8,128)S(1)}, f32[64,256]{1,0:T(8,128)S(1)}, u32[]{:S(2)}, u32[]{:S(2)}) collective-permute-start(f32[64,256]{1,0:T(8,128)S(1)} %get-tuple-element.9), channel_id=1, source_target_pairs={{1,0},{2,1},{3,2},{4,3},{5,4},{6,5},{7,6},{8,7},{9,8},{10,9},{11,1... | collective-permute-start | bytes 196616 | tf_op jit(solution)/shard_map/ppermute | solution.py:15
where the time goes:
time: 587 us; the launch traced here: 586 us
  blocking collectives  498 us (85%)
  starting transfers between devices  42.4 us (7%)
  waiting for transfers between devices  31.3 us (5%)
  matrix products  7.69 us (1%)
    psum x2, blocking collectives, assemble_corners(): return lax.psum(scattered, ('gx', 'gy'))  200 us
    psum x2, blocking collectives, residual_sum(): return lax.psum(jnp.sum(residual * smoothed, axis=1), ('gx', 'gy'))  198 us
    psum x1, blocking collectives, on_device(): curvature = lax.psum(jnp.sum(search * fresh_image, axis=1), ('gx', 'gy'))  99.9 us
    ppermute x16, starting transfers between devices, passed_along(): return lax.ppermute(block, axis, route)  42.4 us
    ppermute x16, waiting for transfers between devices, passed_along(): return lax.ppermute(block, axis, route)  31.3 us
  transfers between devices with their start and end apart: 16, of which 10 were waited for; matrix products, arithmetic and copies ran while one was open for 1% of the time, Pallas kernels for 0%

commit v1 on v0

v1 whole, which is shorter than its diff:
```python
import functools

import jax
import jax.numpy as jnp
from jax import lax
from jax.experimental import pallas as pl
from jax.experimental.pallas import tpu as pltpu
from jax.sharding import PartitionSpec as P

MESH = pl.DeviceIdType.MESH
F32 = jnp.float32
BF16 = jnp.bfloat16
FD = 256
R = 64
LANES = 128


def split_rows(x):
    hi = x.astype(BF16)
    lo = (x - hi.astype(F32)).astype(BF16)
    return jnp.concatenate([hi, lo], axis=0)


def kernel(
    gx_n, gy_n,
    f_hbm, s_hbm, a_hbm, modes_hbm, map_smem, cnt_smem, cinv_hbm,
    x_out, r_out,
    s_v, a_v, cinv_v, f_v, modes_v,
    stat_v, hf_v, hm_v, hs_v,
    wsend, wrecv, xz_v, xq_v, xu_v, oe_v, cs_v, dsm_v,
    t_v, t16_v, g1_v, g2_v, g3src_v, g3_v, y_v, a8_v,
    lsem, hsend, hrecv, wssem, wrsem, gssem, grsem,
):
    sx = lax.axis_index("gx")
    cy = lax.axis_index("gy")
    rg = R // gy_n
    rows_per_group = LANES // gy_n
    groups = gx_n // rows_per_group
    up_x = lax.rem(sx + 1, gx_n)
    dn_x = lax.rem(sx + gx_n - 1, gx_n)
    up_y = lax.rem(cy + 1, gy_n)
    dn_y = lax.rem(cy + gy_n - 1, gy_n)

    loads = [
        pltpu.make_async_copy(f_hbm.at[0, 0], f_v, lsem.at[0]),
        pltpu.make_async_copy(modes_hbm.at[0, 0], modes_v, lsem.at[1]),
        pltpu.make_async_copy(s_hbm.at[0, 0], s_v, lsem.at[2]),
        pltpu.make_async_copy(cinv_hbm, cinv_v, lsem.at[3]),
        pltpu.make_async_copy(a_hbm.at[0, 0], a_v, lsem.at[4]),
    ]
    for load in loads:
        load.start()

    barrier = pltpu.get_barrier_semaphore()

    def greet_row(i, carry):
        pl.semaphore_signal(barrier, inc=1, device_id=(sx, lax.rem(cy + i, gy_n)), device_id_type=MESH)
        return carry

    def greet_column(i, carry):
        pl.semaphore_signal(barrier, inc=1, device_id=(lax.rem(sx + i, gx_n), cy), device_id_type=MESH)
        return carry

    lax.fori_loop(1, gy_n, greet_row, 0)
    lax.fori_loop(1, gx_n, greet_column, 0)

    lane = lax.broadcasted_iota(jnp.int32, (8, FD), 1)
    sub = lax.broadcasted_iota(jnp.int32, (8, FD), 0)
    map_tile = jnp.zeros((8, FD), jnp.int32)
    for k in range(8):
        map_tile = jnp.where(sub == k, map_smem[0, 0, k], map_tile)
    map_tile = lax.rem(map_tile, LANES).astype(F32)
    live_x = jnp.logical_and(lane < cnt_smem[0, 0, 0], sx < gx_n - 1)
    live_y = jnp.logical_and(lane < cnt_smem[0, 0, 1], cy < gy_n - 1)
    for face, live in ((0, live_x), (1, live_y)):
        stat_v[face, 0:8, :] = map_tile
        stat_v[face, 8:16, :] = jnp.where(live, 1.0, 0.0).astype(F32)

    pl.semaphore_wait(barrier, gy_n + gx_n - 2)

    halo = []
    for face, target in ((0, (up_x, cy)), (1, (sx, up_y))):
        cols = pl.ds(face * FD, FD)
        for n, (src, dst) in enumerate((
            (stat_v.at[face], hs_v.at[face]),
            (modes_hbm.at[0, 0, :, cols], hm_v.at[face]),
            (f_hbm.at[0, 0, :, cols], hf_v.at[face]),
        )):
            copy = pltpu.make_async_remote_copy(
                src_ref=src, dst_ref=dst, send_sem=hsend.at[face, n], recv_sem=hrecv.at[face, n],
                device_id=target, device_id_type=MESH,
            )
            copy.start()
            halo.append(copy)

    sub_l = lax.broadcasted_iota(jnp.int32, (LANES, FD), 0).astype(F32)

    def basis_block(block, maps, modes):
        total = jnp.zeros((LANES, FD), F32)
        for k in range(8):
            total = total + jnp.where(sub_l == maps[k : k + 1, :], modes[k : k + 1, :], 0.0)
        hi = total.astype(BF16)
        cols = slice(block * FD, (block + 1) * FD)
        oe_v[0:LANES, cols] = hi
        oe_v[LANES:, cols] = (total - hi.astype(F32)).astype(BF16)

    def own_live(face):
        return stat_v[face, 8:9, :]

    def all_live(block):
        face = block // 2
        if block % 2:
            return stat_v[face, 8:9, :]
        inside = (sx > 0) if face == 0 else (cy > 0)
        return jnp.where(inside, hs_v[face, 8:9, :], 0.0)

    def scatter_rows(n, tile):
        t_v[...] = tile
        for i in range(gy_n):
            t16_v[n, i] = t_v[i * rg : (i + 1) * rg, :]
        g1_v[n, cy] = t16_v[n, cy]

        def send(i, carry):
            to = lax.rem(cy + i, gy_n)
            pltpu.make_async_remote_copy(
                src_ref=t16_v.at[n, to], dst_ref=g1_v.at[n, cy], send_sem=gssem.at[n, 0], recv_sem=grsem.at[n, 0],
                device_id=(sx, to), device_id_type=MESH,
            ).start()
            return carry

        lax.fori_loop(1, gy_n, send, 0)

    def wait_all(ref, n, phase, recv):
        copy = pltpu.make_async_remote_copy(
            src_ref=ref, dst_ref=ref, send_sem=gssem.at[n, phase], recv_sem=grsem.at[n, phase],
            device_id=(sx, up_y), device_id_type=MESH,
        )
        if recv:
            copy.wait_recv()
        else:
            copy.wait_send()

    def gather_columns(n):
        wait_all(g1_v.at[n, pl.ds(0, gy_n - 1)], n, 0, True)
        total = g1_v[n, 0]
        for i in range(1, gy_n):
            total = total + g1_v[n, i]
        g2_v[n, sx] = total

        def send(i, carry):
            pltpu.make_async_remote_copy(
                src_ref=g2_v.at[n, sx], dst_ref=g2_v.at[n, sx], send_sem=gssem.at[n, 1], recv_sem=grsem.at[n, 1],
                device_id=(lax.rem(sx + i, gx_n), cy), device_id_type=MESH,
            ).start()
            return carry

        lax.fori_loop(1, gx_n, send, 0)

    def wait_columns(n):
        wait_all(g2_v.at[n, pl.ds(0, gx_n - 1)], n, 1, True)

    def give_rows(n, tile):
        g3_v[n, cy] = tile

        def send(i, carry):
            pltpu.make_async_remote_copy(
                src_ref=g3_v.at[n, cy], dst_ref=g3_v.at[n, cy], send_sem=gssem.at[n, 2], recv_sem=grsem.at[n, 2],
                device_id=(sx, lax.rem(cy + i, gy_n)), device_id_type=MESH,
            ).start()
            return carry

        lax.fori_loop(1, gy_n, send, 0)

    def take_rows(n):
        wait_all(g3_v.at[n, pl.ds(0, gy_n - 1)], n, 2, True)
        for i in range(gy_n):
            y_v[i * rg : (i + 1) * rg, :] = g3_v[n, i]
        return y_v[...]

    lane_g = lax.broadcasted_iota(jnp.int32, (rg, LANES), 1)

    def solve(n):
        wait_columns(n)
        for g in range(groups):
            base = g * rows_per_group
            last = base + rows_per_group - 1
            total = jnp.where(lane_g < LANES - gy_n, g2_v[n, base], 0.0)
            total = total + jnp.where(lane_g >= gy_n, g2_v[n, last], 0.0)
            for z in range(base + 1, last):
                total = total + g2_v[n, z]
            if g > 0:
                total = total + jnp.where(lane_g < gy_n, g2_v[n, base - 1], 0.0)
            if g < groups - 1:
                total = total + jnp.where(lane_g >= LANES - gy_n, g2_v[n, last + 1], 0.0)
            hi = total.astype(BF16).astype(F32)
            cols = slice(g * LANES, (g + 1) * LANES)
            a8_v[0:rg, cols] = hi
            a8_v[rg : 2 * rg, cols] = total - hi
        res = jnp.dot(a8_v[...].astype(BF16), cs_v[...], preferred_element_type=F32)
        g3src_v[...] = res
        give_rows(n, g3src_v[0:rg, :] + g3src_v[rg : 2 * rg, :])

    def restrict(xx, basis):
        t4 = lax.dot_general(xx, basis, (((1,), (1,)), ((), ())), preferred_element_type=F32)
        return (t4[:R, :LANES] + t4[R:, LANES:]) + (t4[R:, :LANES] + t4[:R, LANES:])

    def prolong(n):
        y = take_rows(n)
        hi = y.astype(BF16)
        lo = (y - hi.astype(F32)).astype(BF16)
        both = jnp.concatenate([jnp.concatenate([hi, hi], axis=1), jnp.concatenate([lo, lo], axis=1)], axis=0)
        return both

    def prolong_block(both, block):
        out = jnp.dot(both, oe_v[:, block * FD : (block + 1) * FD], preferred_element_type=F32)
        return out[:R] + out[R:]

    targets = {0: (dn_x, cy), 1: (up_x, cy), 2: (sx, dn_y), 3: (sx, up_y)}

    def face_copy(op, block):
        return pltpu.make_async_remote_copy(
            src_ref=wsend.at[op, block], dst_ref=wrecv.at[op, block ^ 1],
            send_sem=wssem.at[op, block], recv_sem=wrsem.at[op, block ^ 1],
            device_id=targets[block], device_id_type=MESH,
        )

    def apply(op, xx, matrix, order=(0, 1, 2, 3), send=(0, 1, 2, 3)):
        for block in order:
            out = jnp.dot(xx, matrix[:, block * FD : (block + 1) * FD], preferred_element_type=F32)
            wsend[op, block] = out[:R] + out[R:]
            if block in send:
                face_copy(op, block).start()

    def collected(op, block):
        return jnp.where(all_live(block) > 0.5, wsend[op, block] - wrecv[op, block], 0.0)

    def wait_faces(op, blocks=(0, 1, 2, 3)):
        for block in blocks:
            face_copy(op, block ^ 1).wait_recv()

    loads[0].wait()
    loads[1].wait()
    r_own = []
    for face in range(2):
        cols = slice(face * FD, (face + 1) * FD)
        live = own_live(face)
        r_own.append(jnp.where(live > 0.5, f_v[:, cols], 0.0))
        basis_block(2 * face + 1, stat_v[face, 0:8, :], modes_v[:, cols] * live)
    basis_own = jnp.concatenate([oe_v[:, FD : 2 * FD], oe_v[:, 3 * FD :]], axis=1)
    scatter_rows(0, restrict(split_rows(jnp.concatenate(r_own, axis=1)), basis_own))

    halo[0].wait_recv()
    halo[1].wait_recv()
    halo[3].wait_recv()
    halo[4].wait_recv()
    for face in range(2):
        basis_block(2 * face, hs_v[face, 0:8, :], -(hm_v[face] * all_live(2 * face)))
    halo[2].wait_recv()
    halo[5].wait_recv()
    x0 = jnp.concatenate(
        [
            -jnp.where(all_live(0) > 0.5, hf_v[0], 0.0),
            r_own[0],
            -jnp.where(all_live(2) > 0.5, hf_v[1], 0.0),
            r_own[1],
        ],
        axis=1,
    )
    loads[2].wait()
    apply(0, split_rows(x0), s_v)
    gather_columns(0)

    loads[3].wait()
    lane_c = lax.broadcasted_iota(jnp.int32, (1, LANES), 1)
    cs = jnp.zeros((groups * LANES, LANES), BF16)
    for g in range(groups):
        row = g * rows_per_group + lane_c // gy_n
        near = jnp.logical_and(row >= sx - 1, row <= sx + 1)
        near = jnp.where(near, 1.0, 0.0).astype(BF16)
        cs = cs + cinv_v[:, g * LANES : (g + 1) * LANES] * near
    cs_v[...] = cs

    solve(0)
    both = prolong(0)
    coarse = [prolong_block(both, block) for block in range(4)]
    wait_faces(0)
    for block in range(4):
        xz_v[:, block * FD : (block + 1) * FD] = 0.25 * collected(0, block) + coarse[block]

    loads[4].wait()
    apply(1, split_rows(xz_v[...]), a_v)
    w0 = jnp.concatenate([wsend[1, block] for block in range(4)], axis=1)
    scatter_rows(1, restrict(split_rows(w0), oe_v[...]))

    def owned_dot(a, b):
        return jnp.sum(a[0] * b[0], axis=1, keepdims=True) + jnp.sum(a[1] * b[1], axis=1, keepdims=True)

    def owned(ref):
        return ref[:, FD : 2 * FD], ref[:, 3 * FD :]

    gamma0 = owned_dot(r_own, owned(xz_v))
    delta0 = jnp.sum(xz_v[...] * w0, axis=1, keepdims=True)

    wait_faces(1)
    for block in range(4):
        xq_v[:, block * FD : (block + 1) * FD] = collected(1, block)
    apply(2, split_rows(xq_v[...]), s_v)
    gather_columns(1)
    solve(1)
    both = prolong(1)
    coarse = [prolong_block(both, block) for block in range(4)]
    wait_faces(2)
    for block in range(4):
        xu_v[:, block * FD : (block + 1) * FD] = 0.25 * collected(2, block) + coarse[block]

    apply(3, split_rows(xu_v[...]), a_v, order=(0, 2, 1, 3), send=(0, 2))
    wu = jnp.concatenate([wsend[3, block] for block in range(4)], axis=1)
    sums = (
        gamma0,
        delta0,
        owned_dot(r_own, owned(xu_v)),
        owned_dot(owned(xq_v), owned(xu_v)),
        jnp.sum(xz_v[...] * wu + xu_v[...] * w0, axis=1, keepdims=True),
        jnp.sum(xu_v[...] * wu, axis=1, keepdims=True),
    )
    lane_r = lax.broadcasted_iota(jnp.int32, (R, LANES), 1)
    tile = jnp.zeros((R, LANES), F32)
    for j, value in enumerate(sums):
        tile = jnp.where(lane_r == j, value, tile)
    scatter_rows(2, tile)
    gather_columns(2)
    wait_columns(2)
    total = g2_v[2, 0]
    for i in range(1, gx_n):
        total = total + g2_v[2, i]
    give_rows(2, total)
    wait_faces(3, (1, 3))
    scalars = take_rows(2)
    g0, d0, ru, qu, cross, uu = (scalars[:, j : j + 1] for j in range(6))
    alpha0 = g0 / d0
    g1 = alpha0 * (alpha0 * qu - ru)
    beta1 = 1.0 + g1 / g0
    d1 = beta1 * (beta1 * d0 - alpha0 * cross) + alpha0 * alpha0 * uu
    alpha1 = g1 / d1
    first = alpha0 + alpha1 * beta1
    second = alpha0 * alpha1
    for face in range(2):
        block = 2 * face + 1
        cols = slice(face * FD, (face + 1) * FD)
        own = slice(block * FD, (block + 1) * FD)
        x_out[0, 0, :, cols] = first * xz_v[:, own] - second * xu_v[:, own]
        r_out[0, 0, :, cols] = r_own[face] - first * xq_v[:, own] + second * collected(3, block)

    for copy in halo:
        copy.wait_send()
    for op in range(4):
        for block in (0, 1, 2, 3) if op < 3 else (0, 2):
            face_copy(op, block).wait_send()
    for n in range(3):
        wait_all(t16_v.at[n, pl.ds(0, gy_n - 1)], n, 0, False)
        wait_all(g2_v.at[n, pl.ds(0, gx_n - 1)], n, 1, False)
        wait_all(g3_v.at[n, pl.ds(0, gy_n - 1)], n, 2, False)


def on_device(mesh_shape, forcing_terms, schur, flexibility, coarse_modes, coarse_map, face_slot_count, coarse_inverse):
    gx_n, gy_n = mesh_shape
    rg = R // gy_n
    nb = 4 * FD
    hbm = pl.BlockSpec(memory_space=pl.ANY)
    smem = pl.BlockSpec(memory_space=pltpu.SMEM)
    vmem = pl.BlockSpec(memory_space=pltpu.VMEM)
    out = jax.ShapeDtypeStruct(forcing_terms.shape, F32)
    return pl.pallas_call(
        functools.partial(kernel, gx_n, gy_n),
        out_shape=(out, out),
        in_specs=[hbm, hbm, hbm, hbm, smem, smem, hbm],
        out_specs=(vmem, vmem),
        scratch_shapes=[
            pltpu.VMEM((nb, nb), BF16),
            pltpu.VMEM((nb, nb), BF16),
            pltpu.VMEM(coarse_inverse.shape, BF16),
            pltpu.VMEM((R, 2 * FD), F32),
            pltpu.VMEM((8, 2 * FD), F32),
            pltpu.VMEM((2, 16, FD), F32),
            pltpu.VMEM((2, R, FD), F32),
            pltpu.VMEM((2, 8, FD), F32),
            pltpu.VMEM((2, 16, FD), F32),
            pltpu.VMEM((4, 4, R, FD), F32),
            pltpu.VMEM((4, 4, R, FD), F32),
            pltpu.VMEM((R, nb), F32),
            pltpu.VMEM((R, nb), F32),
            pltpu.VMEM((R, nb), F32),
            pltpu.VMEM((2 * LANES, nb), BF16),
            pltpu.VMEM((gx_n * gy_n, LANES), BF16),
            pltpu.VMEM((8, LANES), F32),
            pltpu.VMEM((R, LANES), F32),
            pltpu.VMEM((3, gy_n, rg, LANES), F32),
            pltpu.VMEM((3, gy_n, rg, LANES), F32),
            pltpu.VMEM((3, gx_n, rg, LANES), F32),
            pltpu.VMEM((2 * rg, LANES), F32),
            pltpu.VMEM((3, gy_n, rg, LANES), F32),
            pltpu.VMEM((R, LANES), F32),
            pltpu.VMEM((2 * rg, gx_n * gy_n), F32),
            pltpu.SemaphoreType.DMA((5,)),
            pltpu.SemaphoreType.DMA((2, 3)),
            pltpu.SemaphoreType.DMA((2, 3)),
            pltpu.SemaphoreType.DMA((4, 4)),
            pltpu.SemaphoreType.DMA((4, 4)),
            pltpu.SemaphoreType.DMA((3, 3)),
            pltpu.SemaphoreType.DMA((3, 3)),
        ],
        compiler_params=pltpu.CompilerParams(
            collective_id=0, has_side_effects=True, vmem_limit_bytes=56 * 1024 * 1024
        ),
    )(forcing_terms, schur, flexibility, coarse_modes, coarse_map, face_slot_count, coarse_inverse)


def solution(mesh):
    shape = (mesh.shape["gx"], mesh.shape["gy"])
    return jax.shard_map(
        functools.partial(on_device, shape),
        mesh=mesh,
        in_specs=(
            P("gx", "gy", None, None),
            P("gx", "gy", None, None),
            P("gx", "gy", None, None),
            P("gx", "gy", None, None),
            P("gx", "gy", None),
            P("gx", "gy", None),
            P(),
        ),
        out_specs=(P("gx", "gy", None, None), P("gx", "gy", None, None)),
        check_vma=False,
    )
```

time: 587 us -> 76.2 us (0.13)
  blocking collectives: 498 us -> 0 us
  Pallas kernels: 0 us -> 72.3 us
  starting transfers between devices: 42.4 us -> 0 us
  waiting for transfers between devices: 31.3 us -> 0 us
  matrix products: 7.69 us -> 0 us
    psum x5 -> x0, blocking collectives: 498 us -> none  [the longest x2 200 us: assemble_corners(): return lax.psum(scattered, ('gx', 'gy'))]
    pallas_call x0 -> x1, Pallas kernels: none -> 72.3 us  [on_device(): pl.pallas_call(functools.partial(kernel, gx_n, gy_n), out_shape=(out, out...]
    ppermute x16 -> x0, starting transfers between devices: 42.4 us -> none  [passed_along(): return lax.ppermute(block, axis, route)]
    ppermute x16 -> x0, waiting for transfers between devices: 31.3 us -> none  [passed_along(): return lax.ppermute(block, axis, route)]
    dot_general x14 -> x0, matrix products: 7.69 us -> none  [the longest x2 2.55 us: on_device(): jnp.dot(distribute_values(search, slot_width), compliance, preferred_elem...]
  transfers between devices with their start and end apart: 16 -> 0, of which waited for: 10 -> 0; matrix products, arithmetic and copies ran while one was open for 1% -> 0% of each run, Pallas kernels for 0% -> 0%
where the time goes in v1:
time: 76.2 us; the launch traced here: 76 us
  Pallas kernels  72.3 us (95%)
  local copies, waits for them, and re-layouts  3.14 us (4%)
    pallas_call x1, Pallas kernels, on_device(): pl.pallas_call(functools.partial(kernel, gx_n, gy_n), out_shape=(out, out...  72.3 us
    unnamed x2, local copies, waits for them, and re-layouts  3.14 us

profile of v1, /device:TPU:1, one launch (start us, length us, event | category | flops | bytes accessed | tf_op | source)
XLA Modules:
  0.0 76.0 jit_solution(4208929613972927969)
XLA Ops:
  0.6 72.3 %shard_map.86 = (f32[1,1,64,512]{3,2,1,0:T(8,128)}, f32[1,1,64,512]{3,2,1,0:T(8,128)}) custom-call(f32[1,1,64,512]{3,2,1,0:T(8,128)} %f_hbm.1, bf16[1,1,1024,1024]{3,2,1,0:T(8,128)(2,1)} %s_hbm.1, bf16[1,1,1024,1024]{3,2,1,0:T(8,128)(2,1)} %a_hbm.1, f32[1,1,8,512]{3,2,1,0:T(8,128)} %modes_hbm.1, s32[1,1,8]{2,1,0:T(1,128)} %map_smem.1, s32[1,1,2]{2,1,0:T(1,128)} %cnt_smem.1, ...), custom_call_target="tpu_custom_call" | custom-call | tf_op jit(solution)/shard_map/pallas_call | solution.py:373
  72.9 1.6 %copy.11 = f32[1,1,64,512]{3,2,1,0:T(8,128)} copy(f32[1,1,64,512]{3,2,1,0:T(8,128)} %get-tuple-element.4) | data formatting | bytes 262144
  74.5 1.6 %copy.12 = f32[1,1,64,512]{3,2,1,0:T(8,128)} copy(f32[1,1,64,512]{3,2,1,0:T(8,128)} %get-tuple-element.5) | data formatting | bytes 262144

commit v2 on v1

v2 whole, which is shorter than its diff:
```python
import functools

import jax
import jax.numpy as jnp
from jax import lax
from jax.experimental import pallas as pl
from jax.experimental.pallas import tpu as pltpu
from jax.sharding import PartitionSpec as P

MESH = pl.DeviceIdType.MESH
F32 = jnp.float32
BF16 = jnp.bfloat16
FD = 256
R = 64
LANES = 128
OFFSETS = ((0, 0), (0, 1), (1, 0), (1, 1), (-1, 0), (-1, 1), (0, -1), (1, -1))


def split_rows(x):
    hi = x.astype(BF16)
    lo = (x - hi.astype(F32)).astype(BF16)
    return jnp.concatenate([hi, lo], axis=0)


def corner_shift(j, columns):
    shift = jnp.zeros_like(j)
    for n, (a, b) in enumerate(OFFSETS):
        shift = jnp.where(j == n, a * columns + b, shift)
    return shift


def kernel(
    gx_n, gy_n,
    f_hbm, s_hbm, a_hbm, modes_hbm, map_smem, cnt_smem, cinv_hbm,
    x_out, r_out,
    s_v, a_v, cinv_v, f_v, modes_v,
    stat_v, hf_v, hm_v, hs_v,
    wsend, wrecv, xz_v, xq_v, xu_v, oe_v, oe2_v, q_v,
    g1_v, part_v, g2_v,
    lsem, hsend, hrecv, wssem, wrsem, gssem, grsem,
):
    sx = lax.axis_index("gx")
    cy = lax.axis_index("gy")
    corners = gx_n * gy_n
    up_x = lax.rem(sx + 1, gx_n)
    dn_x = lax.rem(sx + gx_n - 1, gx_n)
    up_y = lax.rem(cy + 1, gy_n)
    dn_y = lax.rem(cy + gy_n - 1, gy_n)

    loads = [
        pltpu.make_async_copy(f_hbm.at[0, 0], f_v, lsem.at[0]),
        pltpu.make_async_copy(modes_hbm.at[0, 0], modes_v, lsem.at[1]),
        pltpu.make_async_copy(cinv_hbm, cinv_v, lsem.at[2]),
        pltpu.make_async_copy(s_hbm.at[0, 0], s_v, lsem.at[3]),
        pltpu.make_async_copy(a_hbm.at[0, 0], a_v, lsem.at[4]),
    ]
    for load in loads:
        load.start()

    def each_row(send):
        half = gy_n // 2
        send(lax.rem(cy + half, gy_n))

        def pair(i, carry):
            send(lax.rem(cy + half + i, gy_n))
            send(lax.rem(cy + half - i, gy_n))
            return carry

        lax.fori_loop(1, half, pair, 0)

    def each_column(send):
        x_n, z_n = 4, gx_n // 4
        half = z_n // 2
        x_at, z_at = sx // z_n, lax.rem(sx, z_n)

        def level(dz, shifts=(2, 1, 3, 0)):
            z_to = lax.rem(z_at + dz, z_n)
            for dx in shifts:
                send(lax.rem(x_at + dx, x_n) * z_n + z_to)

        level(half)

        def pair(i, carry):
            level(half + i)
            level(half - i)
            return carry

        lax.fori_loop(1, half, pair, 0)
        level(0, (2, 1, 3))

    barrier = pltpu.get_barrier_semaphore()

    def greet(target):
        pl.semaphore_signal(barrier, inc=1, device_id=target, device_id_type=MESH)

    each_column(lambda to: greet((to, cy)))
    each_row(lambda to: greet((sx, to)))

    lane = lax.broadcasted_iota(jnp.int32, (8, FD), 1)
    sub = lax.broadcasted_iota(jnp.int32, (8, FD), 0)
    map_tile = jnp.zeros((8, FD), jnp.int32)
    for k in range(8):
        map_tile = jnp.where(sub == k, map_smem[0, 0, k], map_tile)
    map_tile = map_tile.astype(F32)
    live_x = jnp.logical_and(lane < cnt_smem[0, 0, 0], sx < gx_n - 1)
    live_y = jnp.logical_and(lane < cnt_smem[0, 0, 1], cy < gy_n - 1)
    for face, live in ((0, live_x), (1, live_y)):
        stat_v[face, 0:8, :] = map_tile
        stat_v[face, 8:16, :] = jnp.where(live, 1.0, 0.0).astype(F32)

    corner = (sx * gy_n + cy + corner_shift(sub, gy_n)).astype(F32)

    def basis_block(block, maps, modes):
        total = jnp.zeros((8, FD), F32)
        for k in range(8):
            total = total + jnp.where(corner == maps[k : k + 1, :], modes[k : k + 1, :], 0.0)
        hi = total.astype(BF16).astype(F32)
        lo = total - hi
        cols = slice(block * FD, (block + 1) * FD)
        oe_v[:, cols] = jnp.concatenate([hi, lo], axis=0).astype(BF16)
        oe2_v[:, cols] = jnp.concatenate([hi, hi, lo, lo], axis=0).astype(BF16)

    def own_live(face):
        return stat_v[face, 8:9, :]

    def all_live(block):
        face = block // 2
        if block % 2:
            return stat_v[face, 8:9, :]
        inside = (sx > 0) if face == 0 else (cy > 0)
        return jnp.where(inside, hs_v[face, 8:9, :], 0.0)

    def row_send(n, tile):
        g1_v[n, cy] = tile

        def send(to):
            pltpu.make_async_remote_copy(
                src_ref=g1_v.at[n, cy], dst_ref=g1_v.at[n, cy], send_sem=gssem.at[n, 0], recv_sem=grsem.at[n, 0],
                device_id=(sx, to), device_id_type=MESH,
            ).start()

        each_row(send)

    def column_send(n, source):
        def send(to):
            pltpu.make_async_remote_copy(
                src_ref=source(to), dst_ref=g2_v.at[n, sx], send_sem=gssem.at[n, 1], recv_sem=grsem.at[n, 1],
                device_id=(to, cy), device_id_type=MESH,
            ).start()

        each_column(send)

    def wait_all(ref, n, phase, recv):
        copy = pltpu.make_async_remote_copy(
            src_ref=ref, dst_ref=ref, send_sem=gssem.at[n, phase], recv_sem=grsem.at[n, phase],
            device_id=(sx, up_y), device_id_type=MESH,
        )
        if recv:
            copy.wait_recv()
        else:
            copy.wait_send()

    def wait_row(n):
        wait_all(g1_v.at[n, pl.ds(0, gy_n - 1)], n, 0, True)

    def wait_column(n):
        wait_all(g2_v.at[n, pl.ds(0, gx_n - 1)], n, 1, True)

    def tree(values):
        while len(values) > 1:
            values = [a + b for a, b in zip(values[::2], values[1::2])]
        return values[0]

    def restrict(xx, basis):
        t = lax.dot_general(basis, xx, (((1,), (1,)), ((), ())), preferred_element_type=F32)
        t = t[0:8] + t[8:16]
        return t + pltpu.roll(t, R, 1)

    lane_g = lax.broadcasted_iota(jnp.int32, (LANES, LANES), 1)

    def solve(n):
        wait_row(n)
        sums = g1_v[n].reshape(LANES, LANES)
        hi = sums.astype(BF16).astype(F32)
        terms = jnp.where(lane_g < R, hi, sums - hi).astype(BF16)
        part = jnp.dot(q_v[...], terms, preferred_element_type=F32)
        part_v[n] = part.reshape(gx_n, 8, LANES)
        g2_v[n, sx] = part_v[n, sx]
        column_send(n, lambda to: part_v.at[n, to])

    def prolong(n):
        wait_column(n)
        y = tree([g2_v[n, i] for i in range(gx_n)])
        y = y + pltpu.roll(y, R, 1)
        hi = y.astype(BF16).astype(F32)
        lo = y - hi
        terms = jnp.concatenate([hi, lo, hi, lo], axis=0)
        return jnp.transpose(terms)[:R].astype(BF16)

    def prolong_block(terms, block):
        return jnp.dot(terms, oe2_v[:, block * FD : (block + 1) * FD], preferred_element_type=F32)

    targets = {0: (dn_x, cy), 1: (up_x, cy), 2: (sx, dn_y), 3: (sx, up_y)}

    def face_copy(op, block):
        return pltpu.make_async_remote_copy(
            src_ref=wsend.at[op, block], dst_ref=wrecv.at[op, block ^ 1],
            send_sem=wssem.at[op, block], recv_sem=wrsem.at[op, block ^ 1],
            device_id=targets[block], device_id_type=MESH,
        )

    def apply(op, xx, matrix, order=(0, 1, 2, 3), send=(0, 1, 2, 3)):
        for block in order:
            out = jnp.dot(xx, matrix[:, block * FD : (block + 1) * FD], preferred_element_type=F32)
            wsend[op, block] = out[:R] + out[R:]
            if block in send:
                face_copy(op, block).start()

    def collected(op, block):
        return jnp.where(all_live(block) > 0.5, wsend[op, block] - wrecv[op, block], 0.0)

    def wait_faces(op, blocks=(0, 1, 2, 3)):
        for block in blocks:
            face_copy(op, block ^ 1).wait_recv()

    loads[0].wait()
    loads[1].wait()
    r_own = []
    for face in range(2):
        cols = slice(face * FD, (face + 1) * FD)
        live = own_live(face)
        r_own.append(jnp.where(live > 0.5, f_v[:, cols], 0.0))
        basis_block(2 * face + 1, stat_v[face, 0:8, :], modes_v[:, cols] * live)
    basis_own = jnp.concatenate([oe_v[:, FD : 2 * FD], oe_v[:, 3 * FD :]], axis=1)
    first_sums = restrict(split_rows(jnp.concatenate(r_own, axis=1)), basis_own)

    pl.semaphore_wait(barrier, gy_n + gx_n - 2)

    row_send(0, first_sums)
    halo = []
    for face, target in ((0, (up_x, cy)), (1, (sx, up_y))):
        cols = pl.ds(face * FD, FD)
        for n, (src, dst) in enumerate((
            (stat_v.at[face], hs_v.at[face]),
            (modes_v.at[:, cols], hm_v.at[face]),
            (f_v.at[:, cols], hf_v.at[face]),
        )):
            copy = pltpu.make_async_remote_copy(
                src_ref=src, dst_ref=dst, send_sem=hsend.at[face, n], recv_sem=hrecv.at[face, n],
                device_id=target, device_id_type=MESH,
            )
            copy.start()
            halo.append(copy)

    loads[2].wait()
    row_q = lax.broadcasted_iota(jnp.int32, (8 * gx_n, LANES), 0)
    lane_q = lax.broadcasted_iota(jnp.int32, (8 * gx_n, LANES), 1)
    at = (row_q // 8) * gy_n + cy + corner_shift(lax.rem(row_q, 8), gy_n) - lane_q
    pick = [jnp.where(at == g * LANES, 1.0, 0.0).astype(BF16) for g in range(corners // LANES)]
    to_column = lax.dot_general(
        jnp.concatenate(pick, axis=1), cinv_v[...], (((1,), (1,)), ((), ())), preferred_element_type=F32
    ).astype(BF16)
    row_p = lax.broadcasted_iota(jnp.int32, (8 * gy_n, LANES), 0)
    lane_p = lax.broadcasted_iota(jnp.int32, (8 * gy_n, LANES), 1)
    at = sx * gy_n + row_p // 8 + corner_shift(lax.rem(row_p, 8), gy_n) - lane_p
    pick = [jnp.where(at == g * LANES, 1.0, 0.0).astype(BF16) for g in range(corners // LANES)]
    q_v[...] = lax.dot_general(
        to_column, jnp.concatenate(pick, axis=1), (((1,), (1,)), ((), ())), preferred_element_type=F32
    ).astype(BF16)

    halo[2].wait_recv()
    halo[5].wait_recv()
    halo[0].wait_recv()
    halo[3].wait_recv()
    x0 = jnp.concatenate(
        [
            -jnp.where(all_live(0) > 0.5, hf_v[0], 0.0),
            r_own[0],
            -jnp.where(all_live(2) > 0.5, hf_v[1], 0.0),
            r_own[1],
        ],
        axis=1,
    )
    loads[3].wait()
    apply(0, split_rows(x0), s_v)
    solve(0)

    halo[1].wait_recv()
    halo[4].wait_recv()
    for face in range(2):
        basis_block(2 * face, hs_v[face, 0:8, :], -(hm_v[face] * all_live(2 * face)))

    wait_faces(0)
    for block in range(4):
        xz_v[:, block * FD : (block + 1) * FD] = 0.25 * collected(0, block)
    loads[4].wait()
    terms = prolong(0)
    for block in range(4):
        xz_v[:, block * FD : (block + 1) * FD] += prolong_block(terms, block)

    apply(1, split_rows(xz_v[...]), a_v)
    w0 = jnp.concatenate([wsend[1, block] for block in range(4)], axis=1)
    row_send(1, restrict(split_rows(w0), oe_v[...]))

    def owned_dot(a, b):
        return jnp.sum(a[0] * b[0], axis=1, keepdims=True) + jnp.sum(a[1] * b[1], axis=1, keepdims=True)

    def owned(ref):
        return ref[:, FD : 2 * FD], ref[:, 3 * FD :]

    gamma0 = owned_dot(r_own, owned(xz_v))
    delta0 = jnp.sum(xz_v[...] * w0, axis=1, keepdims=True)

    wait_faces(1)
    for block in range(4):
        xq_v[:, block * FD : (block + 1) * FD] = collected(1, block)
    apply(2, split_rows(xq_v[...]), s_v)
    solve(1)
    wait_faces(2)
    for block in range(4):
        xu_v[:, block * FD : (block + 1) * FD] = 0.25 * collected(2, block)
    terms = prolong(1)
    for block in range(4):
        xu_v[:, block * FD : (block + 1) * FD] += prolong_block(terms, block)

    apply(3, split_rows(xu_v[...]), a_v, order=(0, 2, 1, 3), send=(0, 2))
    wu = jnp.concatenate([wsend[3, block] for block in range(4)], axis=1)
    sums = (
        gamma0,
        delta0,
        owned_dot(r_own, owned(xu_v)),
        owned_dot(owned(xq_v), owned(xu_v)),
        jnp.sum(xz_v[...] * wu + xu_v[...] * w0, axis=1, keepdims=True),
        jnp.sum(xu_v[...] * wu, axis=1, keepdims=True),
    )
    lane_r = lax.broadcasted_iota(jnp.int32, (LANES, LANES), 1)
    tile = jnp.zeros((LANES, LANES), F32)
    for j, value in enumerate(sums):
        tile = jnp.where(lane_r == j, jnp.concatenate([value, value], axis=0), tile)
    row_send(2, jnp.transpose(tile)[0:8])
    wait_row(2)
    g2_v[2, sx] = tree([g1_v[2, i] for i in range(gy_n)])
    column_send(2, lambda to: g2_v.at[2, sx])
    wait_faces(3, (1, 3))
    wait_column(2)
    scalars = tree([g2_v[2, i] for i in range(gx_n)])
    g0, d0, ru, qu, cross, uu = (scalars[j : j + 1] for j in range(6))
    alpha0 = g0 / d0
    g1 = alpha0 * (alpha0 * qu - ru)
    beta1 = 1.0 + g1 / g0
    d1 = beta1 * (beta1 * d0 - alpha0 * cross) + alpha0 * alpha0 * uu
    alpha1 = g1 / d1
    sub_s = lax.broadcasted_iota(jnp.int32, (8, LANES), 0)
    steps = jnp.where(sub_s == 0, alpha0 + alpha1 * beta1, alpha0 * alpha1)
    steps = jnp.transpose(steps)[:R]
    first, second = steps[:, 0:1], steps[:, 1:2]
    for face in range(2):
        block = 2 * face + 1
        cols = slice(face * FD, (face + 1) * FD)
        own = slice(block * FD, (block + 1) * FD)
        x_out[0, 0, :, cols] = first * xz_v[:, own] - second * xu_v[:, own]
        r_out[0, 0, :, cols] = r_own[face] - first * xq_v[:, own] + second * collected(3, block)

    for copy in halo:
        copy.wait_send()
    for op in range(4):
        for block in (0, 1, 2, 3) if op < 3 else (0, 2):
            face_copy(op, block).wait_send()
    for n in range(3):
        wait_all(g1_v.at[n, pl.ds(0, gy_n - 1)], n, 0, False)
        wait_all(g2_v.at[n, pl.ds(0, gx_n - 1)], n, 1, False)


def on_device(mesh_shape, forcing_terms, schur, flexibility, coarse_modes, coarse_map, face_slot_count, coarse_inverse):
    gx_n, gy_n = mesh_shape
    nb = 4 * FD
    hbm = pl.BlockSpec(memory_space=pl.ANY)
    smem = pl.BlockSpec(memory_space=pltpu.SMEM)
    vmem = pl.BlockSpec(memory_space=pltpu.VMEM)
    out = jax.ShapeDtypeStruct(forcing_terms.shape, F32)
    return pl.pallas_call(
        functools.partial(kernel, gx_n, gy_n),
        out_shape=(out, out),
        in_specs=[hbm, hbm, hbm, hbm, smem, smem, hbm],
        out_specs=(vmem, vmem),
        scratch_shapes=[
            pltpu.VMEM((nb, nb), BF16),
            pltpu.VMEM((nb, nb), BF16),
            pltpu.VMEM(coarse_inverse.shape, BF16),
            pltpu.VMEM((R, 2 * FD), F32),
            pltpu.VMEM((8, 2 * FD), F32),
            pltpu.VMEM((2, 16, FD), F32),
            pltpu.VMEM((2, R, FD), F32),
            pltpu.VMEM((2, 8, FD), F32),
            pltpu.VMEM((2, 16, FD), F32),
            pltpu.VMEM((4, 4, R, FD), F32),
            pltpu.VMEM((4, 4, R, FD), F32),
            pltpu.VMEM((R, nb), F32),
            pltpu.VMEM((R, nb), F32),
            pltpu.VMEM((R, nb), F32),
            pltpu.VMEM((16, nb), BF16),
            pltpu.VMEM((32, nb), BF16),
            pltpu.VMEM((8 * gx_n, 8 * gy_n), BF16),
            pltpu.VMEM((3, gy_n, 8, LANES), F32),
            pltpu.VMEM((2, gx_n, 8, LANES), F32),
            pltpu.VMEM((3, gx_n, 8, LANES), F32),
            pltpu.SemaphoreType.DMA((5,)),
            pltpu.SemaphoreType.DMA((2, 3)),
            pltpu.SemaphoreType.DMA((2, 3)),
            pltpu.SemaphoreType.DMA((4, 4)),
            pltpu.SemaphoreType.DMA((4, 4)),
            pltpu.SemaphoreType.DMA((3, 2)),
            pltpu.SemaphoreType.DMA((3, 2)),
        ],
        compiler_params=pltpu.CompilerParams(
            collective_id=0, has_side_effects=True, vmem_limit_bytes=56 * 1024 * 1024
        ),
    )(forcing_terms, schur, flexibility, coarse_modes, coarse_map, face_slot_count, coarse_inverse)


def solution(mesh):
    shape = (mesh.shape["gx"], mesh.shape["gy"])
    return jax.shard_map(
        functools.partial(on_device, shape),
        mesh=mesh,
        in_specs=(
            P("gx", "gy", None, None),
            P("gx", "gy", None, None),
            P("gx", "gy", None, None),
            P("gx", "gy", None, None),
            P("gx", "gy", None),
            P("gx", "gy", None),
            P(),
        ),
        out_specs=(P("gx", "gy", None, None), P("gx", "gy", None, None)),
        check_vma=False,
    )
```

time: 76.2 us -> 59.7 us (0.78)
  Pallas kernels: 72.3 us -> 55.8 us
    pallas_call x1, Pallas kernels: 72.3 us -> 55.8 us  [on_device(): pl.pallas_call(functools.partial(kernel, gx_n, gy_n), out_shape=(out, out...]
where the time goes in v2:
time: 59.7 us; the launch traced here: 59.6 us
  Pallas kernels  55.8 us (93%)
  local copies, waits for them, and re-layouts  3.14 us (5%)
  between operations  0.64 us (1%)
    pallas_call x1, Pallas kernels, on_device(): pl.pallas_call(functools.partial(kernel, gx_n, gy_n), out_shape=(out, out...  55.8 us
    unnamed x2, local copies, waits for them, and re-layouts  3.14 us

profile of v2, /device:TPU:1, one launch (start us, length us, event | category | flops | bytes accessed | tf_op | source)
XLA Modules:
  0.0 59.6 jit_solution(291574297244694821)
XLA Ops:
  0.6 55.8 %shard_map.86 = (f32[1,1,64,512]{3,2,1,0:T(8,128)}, f32[1,1,64,512]{3,2,1,0:T(8,128)}) custom-call(f32[1,1,64,512]{3,2,1,0:T(8,128)} %f_hbm.1, bf16[1,1,1024,1024]{3,2,1,0:T(8,128)(2,1)} %s_hbm.1, bf16[1,1,1024,1024]{3,2,1,0:T(8,128)(2,1)} %a_hbm.1, f32[1,1,8,512]{3,2,1,0:T(8,128)} %modes_hbm.1, s32[1,1,8]{2,1,0:T(1,128)} %map_smem.1, s32[1,1,2]{2,1,0:T(1,128)} %cnt_smem.1, ...), custom_call_target="tpu_custom_call" | custom-call | tf_op jit(solution)/shard_map/pallas_call | solution.py:381
  56.4 1.6 %copy.11 = f32[1,1,64,512]{3,2,1,0:T(8,128)} copy(f32[1,1,64,512]{3,2,1,0:T(8,128)} %get-tuple-element.4) | data formatting | bytes 262144
  58.0 1.6 %copy.12 = f32[1,1,64,512]{3,2,1,0:T(8,128)} copy(f32[1,1,64,512]{3,2,1,0:T(8,128)} %get-tuple-element.5) | data formatting | bytes 262144

commit v3 on v2

--- a/solution.py
+++ b/solution.py
@@ -32,10 +32,10 @@
 def kernel(
     gx_n, gy_n,
     f_hbm, s_hbm, a_hbm, modes_hbm, map_smem, cnt_smem, cinv_hbm,
-    x_out, r_out,
+    out_v,
     s_v, a_v, cinv_v, f_v, modes_v,
     stat_v, hf_v, hm_v, hs_v,
-    wsend, wrecv, xz_v, xq_v, xu_v, oe_v, oe2_v, q_v,
+    wsend, wrecv, xz_v, xq_v, xu_v, oe_v, oe2_v, oef_v, oef2_v, gram_v, q_v,
     g1_v, part_v, g2_v,
     lsem, hsend, hrecv, wssem, wrsem, gssem, grsem,
 ):
@@ -130,8 +130,18 @@
         inside = (sx > 0) if face == 0 else (cy > 0)
         return jnp.where(inside, hs_v[face, 8:9, :], 0.0)
 
+    lane_8 = lax.broadcasted_iota(jnp.int32, (8, LANES), 1)
+    lane_4 = lax.broadcasted_iota(jnp.int32, (4, LANES), 1)
+
+    def packed(tile):
+        return jnp.where(lane_8 < R, tile, pltpu.roll(tile, 4, 0))[0:4]
+
+    def unpacked(tile):
+        other = pltpu.roll(tile, R, 1)
+        return jnp.concatenate([jnp.where(lane_4 < R, tile, other), jnp.where(lane_4 < R, other, tile)], axis=0)
+
     def row_send(n, tile):
-        g1_v[n, cy] = tile
+        g1_v[n, cy] = packed(tile)
 
         def send(to):
             pltpu.make_async_remote_copy(
@@ -176,29 +186,38 @@
         t = t[0:8] + t[8:16]
         return t + pltpu.roll(t, R, 1)
 
-    lane_g = lax.broadcasted_iota(jnp.int32, (LANES, LANES), 1)
+    lane_g = lax.broadcasted_iota(jnp.int32, (4 * gy_n, LANES), 1)
+    lane_s = lax.broadcasted_iota(jnp.int32, (4 * gx_n, LANES), 1)
 
     def solve(n):
         wait_row(n)
-        sums = g1_v[n].reshape(LANES, LANES)
+        sums = g1_v[n].reshape(4 * gy_n, LANES)
         hi = sums.astype(BF16).astype(F32)
-        terms = jnp.where(lane_g < R, hi, sums - hi).astype(BF16)
+        lo = sums - hi
+        terms = jnp.concatenate(
+            [jnp.where(lane_g < R, hi, pltpu.roll(lo, R, 1)), jnp.where(lane_g < R, pltpu.roll(hi, R, 1), lo)], axis=0
+        ).astype(BF16)
         part = jnp.dot(q_v[...], terms, preferred_element_type=F32)
-        part_v[n] = part.reshape(gx_n, 8, LANES)
+        part = part + pltpu.roll(part, R, 1)
+        part_v[n] = jnp.where(lane_s < R, part[: 4 * gx_n], part[4 * gx_n :]).reshape(gx_n, 4, LANES)
         g2_v[n, sx] = part_v[n, sx]
         column_send(n, lambda to: part_v.at[n, to])
 
-    def prolong(n):
+    def solved(n):
         wait_column(n)
-        y = tree([g2_v[n, i] for i in range(gx_n)])
-        y = y + pltpu.roll(y, R, 1)
+        return unpacked(tree([g2_v[n, i] for i in range(gx_n)]))
+
+    def transposed(y):
         hi = y.astype(BF16).astype(F32)
         lo = y - hi
         terms = jnp.concatenate([hi, lo, hi, lo], axis=0)
         return jnp.transpose(terms)[:R].astype(BF16)
 
-    def prolong_block(terms, block):
-        return jnp.dot(terms, oe2_v[:, block * FD : (block + 1) * FD], preferred_element_type=F32)
+    def coarse_block(terms, ref, block):
+        return jnp.dot(terms, ref[:, block * FD : (block + 1) * FD], preferred_element_type=F32)
+
+    def gram(y):
+        return tree([gram_v[j] * y[j : j + 1, :] for j in range(8)])
 
     targets = {0: (dn_x, cy), 1: (up_x, cy), 2: (sx, dn_y), 3: (sx, up_y)}
 
@@ -209,10 +228,16 @@
             device_id=targets[block], device_id_type=MESH,
         )
 
-    def apply(op, xx, matrix, order=(0, 1, 2, 3), send=(0, 1, 2, 3)):
-        for block in order:
+    def apply(op, xx, matrix, send=True):
+        for block in range(4):
             out = jnp.dot(xx, matrix[:, block * FD : (block + 1) * FD], preferred_element_type=F32)
             wsend[op, block] = out[:R] + out[R:]
+            if send:
+                face_copy(op, block).start()
+
+    def add_coarse(op, terms, order, send):
+        for block in order:
+            wsend[op, block] += coarse_block(terms, oef2_v, block)
             if block in send:
                 face_copy(op, block).start()
 
@@ -255,14 +280,18 @@
     loads[2].wait()
     row_q = lax.broadcasted_iota(jnp.int32, (8 * gx_n, LANES), 0)
     lane_q = lax.broadcasted_iota(jnp.int32, (8 * gx_n, LANES), 1)
-    at = (row_q // 8) * gy_n + cy + corner_shift(lax.rem(row_q, 8), gy_n) - lane_q
+    last_q = row_q >= 4 * gx_n
+    row_q = jnp.where(last_q, row_q - 4 * gx_n, row_q)
+    at = (row_q // 4) * gy_n + cy + corner_shift(lax.rem(row_q, 4) + jnp.where(last_q, 4, 0), gy_n) - lane_q
     pick = [jnp.where(at == g * LANES, 1.0, 0.0).astype(BF16) for g in range(corners // LANES)]
     to_column = lax.dot_general(
         jnp.concatenate(pick, axis=1), cinv_v[...], (((1,), (1,)), ((), ())), preferred_element_type=F32
     ).astype(BF16)
     row_p = lax.broadcasted_iota(jnp.int32, (8 * gy_n, LANES), 0)
     lane_p = lax.broadcasted_iota(jnp.int32, (8 * gy_n, LANES), 1)
-    at = sx * gy_n + row_p // 8 + corner_shift(lax.rem(row_p, 8), gy_n) - lane_p
+    last_p = row_p >= 4 * gy_n
+    row_p = jnp.where(last_p, row_p - 4 * gy_n, row_p)
+    at = sx * gy_n + row_p // 4 + corner_shift(lax.rem(row_p, 4) + jnp.where(last_p, 4, 0), gy_n) - lane_p
     pick = [jnp.where(at == g * LANES, 1.0, 0.0).astype(BF16) for g in range(corners // LANES)]
     q_v[...] = lax.dot_general(
         to_column, jnp.concatenate(pick, axis=1), (((1,), (1,)), ((), ())), preferred_element_type=F32
@@ -289,68 +318,102 @@
     halo[4].wait_recv()
     for face in range(2):
         basis_block(2 * face, hs_v[face, 0:8, :], -(hm_v[face] * all_live(2 * face)))
+    loads[4].wait()
+    basis = oe_v[...]
+    oef = jnp.dot(basis, a_v[...], preferred_element_type=F32)
+    oef = oef[0:8] + oef[8:16]
+    hi = oef.astype(BF16).astype(F32)
+    lo = oef - hi
+    oef_v[...] = jnp.concatenate([hi, lo], axis=0).astype(BF16)
+    oef2_v[...] = jnp.concatenate([hi, hi, lo, lo], axis=0).astype(BF16)
+    square = lax.dot_general(basis, oef_v[...], (((1,), (1,)), ((), ())), preferred_element_type=F32)
+    square = square[0:8] + square[8:16]
+    square = square[:, 0:8] + square[:, 8:16]
+    for j in range(8):
+        gram_v[j] = jnp.broadcast_to(square[:, j : j + 1], (8, LANES))
+
+    def owned_dot(a, b):
+        return jnp.sum(a[0] * b[0], axis=1, keepdims=True) + jnp.sum(a[1] * b[1], axis=1, keepdims=True)
+
+    def owned(ref):
+        return ref[:, FD : 2 * FD], ref[:, 3 * FD :]
+
+    def images(op):
+        return jnp.concatenate([wsend[op, block] for block in range(4)], axis=1)
 
     wait_faces(0)
     for block in range(4):
         xz_v[:, block * FD : (block + 1) * FD] = 0.25 * collected(0, block)
-    loads[4].wait()
-    terms = prolong(0)
+    xx = split_rows(xz_v[...])
+    apply(1, xx, a_v, send=False)
+    fine_sums = restrict(xx, oef_v[...])
+
+    y = solved(0)
+    next_sums = fine_sums + gram(y)
+    row_send(1, next_sums)
+
+    terms = transposed(y)
+    add_coarse(1, terms, (0, 1, 2, 3), (0, 1, 2, 3))
     for block in range(4):
-        xz_v[:, block * FD : (block + 1) * FD] += prolong_block(terms, block)
-
-    apply(1, split_rows(xz_v[...]), a_v)
-    w0 = jnp.concatenate([wsend[1, block] for block in range(4)], axis=1)
-    row_send(1, restrict(split_rows(w0), oe_v[...]))
-
-    def owned_dot(a, b):
-        return jnp.sum(a[0] * b[0], axis=1, keepdims=True) + jnp.sum(a[1] * b[1], axis=1, keepdims=True)
-
-    def owned(ref):
-        return ref[:, FD : 2 * FD], ref[:, 3 * FD :]
-
+        xz_v[:, block * FD : (block + 1) * FD] += coarse_block(terms, oe2_v, block)
+    w0 = images(1)
     gamma0 = owned_dot(r_own, owned(xz_v))
     delta0 = jnp.sum(xz_v[...] * w0, axis=1, keepdims=True)
 
     wait_faces(1)
     for block in range(4):
         xq_v[:, block * FD : (block + 1) * FD] = collected(1, block)
-    apply(2, split_rows(xq_v[...]), s_v)
+    xx = split_rows(xq_v[...])
+    apply(2, xx, s_v)
     solve(1)
+    image_sums = restrict(jnp.concatenate([xx[:, FD : 2 * FD], xx[:, 3 * FD :]], axis=1), basis_own)
+
     wait_faces(2)
     for block in range(4):
         xu_v[:, block * FD : (block + 1) * FD] = 0.25 * collected(2, block)
-    terms = prolong(1)
-    for block in range(4):
-        xu_v[:, block * FD : (block + 1) * FD] += prolong_block(terms, block)
-
-    apply(3, split_rows(xu_v[...]), a_v, order=(0, 2, 1, 3), send=(0, 2))
-    wu = jnp.concatenate([wsend[3, block] for block in range(4)], axis=1)
+    xx = split_rows(xu_v[...])
+    apply(3, xx, a_v, send=False)
+    smoothed_sums = restrict(xx, oef_v[...])
+    wv = images(3)
     sums = (
         gamma0,
         delta0,
         owned_dot(r_own, owned(xu_v)),
         owned_dot(owned(xq_v), owned(xu_v)),
-        jnp.sum(xz_v[...] * wu + xu_v[...] * w0, axis=1, keepdims=True),
-        jnp.sum(xu_v[...] * wu, axis=1, keepdims=True),
+        jnp.sum(xz_v[...] * wv + xu_v[...] * images(1), axis=1, keepdims=True),
+        jnp.sum(xu_v[...] * wv, axis=1, keepdims=True),
     )
     lane_r = lax.broadcasted_iota(jnp.int32, (LANES, LANES), 1)
     tile = jnp.zeros((LANES, LANES), F32)
     for j, value in enumerate(sums):
         tile = jnp.where(lane_r == j, jnp.concatenate([value, value], axis=0), tile)
-    row_send(2, jnp.transpose(tile)[0:8])
+    fine_scalars = jnp.transpose(tile)[0:8]
+
+    y = solved(1)
+    sub_s = lax.broadcasted_iota(jnp.int32, (8, LANES), 0)
+    coarse_scalars = jnp.zeros((8, LANES), F32)
+    for j, factor in (
+        (2, first_sums), (3, image_sums), (4, 2.0 * next_sums), (5, 2.0 * smoothed_sums + gram(y))
+    ):
+        coarse_scalars = jnp.where(sub_s == j, jnp.sum(y * factor, axis=0, keepdims=True), coarse_scalars)
+    row_send(2, fine_scalars + coarse_scalars)
+
+    terms = transposed(y)
+    add_coarse(3, terms, (0, 2, 1, 3), (0, 2))
+    for block in (1, 3):
+        xu_v[:, block * FD : (block + 1) * FD] += coarse_block(terms, oe2_v, block)
     wait_row(2)
     g2_v[2, sx] = tree([g1_v[2, i] for i in range(gy_n)])
     column_send(2, lambda to: g2_v.at[2, sx])
     wait_faces(3, (1, 3))
     wait_column(2)
-    scalars = tree([g2_v[2, i] for i in range(gx_n)])
+    scalars = unpacked(tree([g2_v[2, i] for i in range(gx_n)]))
     g0, d0, ru, qu, cross, uu = (scalars[j : j + 1] for j in range(6))
     alpha0 = g0 / d0
     g1 = alpha0 * (alpha0 * qu - ru)
     beta1 = 1.0 + g1 / g0
     d1 = beta1 * (beta1 * d0 - alpha0 * cross) + alpha0 * alpha0 * uu
     alpha1 = g1 / d1
-    sub_s = lax.broadcasted_iota(jnp.int32, (8, LANES), 0)
     steps = jnp.where(sub_s == 0, alpha0 + alpha1 * beta1, alpha0 * alpha1)
     steps = jnp.transpose(steps)[:R]
     first, second = steps[:, 0:1], steps[:, 1:2]
@@ -358,8 +421,8 @@
         block = 2 * face + 1
         cols = slice(face * FD, (face + 1) * FD)
         own = slice(block * FD, (block + 1) * FD)
-        x_out[0, 0, :, cols] = first * xz_v[:, own] - second * xu_v[:, own]
-        r_out[0, 0, :, cols] = r_own[face] - first * xq_v[:, own] + second * collected(3, block)
+        out_v[0, :, cols] = first * xz_v[:, own] - second * xu_v[:, own]
+        out_v[1, :, cols] = r_own[face] - first * xq_v[:, own] + second * collected(3, block)
 
     for copy in halo:
         copy.wait_send()
@@ -371,18 +434,27 @@
         wait_all(g2_v.at[n, pl.ds(0, gx_n - 1)], n, 1, False)
 
 
+def hand_out(both, x_out, r_out, sem):
+    copies = [
+        pltpu.make_async_copy(both.at[n], ref.at[0, 0], sem.at[n]) for n, ref in enumerate((x_out, r_out))
+    ]
+    for copy in copies:
+        copy.start()
+    for copy in copies:
+        copy.wait()
+
+
 def on_device(mesh_shape, forcing_terms, schur, flexibility, coarse_modes, coarse_map, face_slot_count, coarse_inverse):
     gx_n, gy_n = mesh_shape
     nb = 4 * FD
     hbm = pl.BlockSpec(memory_space=pl.ANY)
     smem = pl.BlockSpec(memory_space=pltpu.SMEM)
     vmem = pl.BlockSpec(memory_space=pltpu.VMEM)
-    out = jax.ShapeDtypeStruct(forcing_terms.shape, F32)
-    return pl.pallas_call(
+    both = pl.pallas_call(
         functools.partial(kernel, gx_n, gy_n),
-        out_shape=(out, out),
+        out_shape=pltpu.VMEM((2, R, 2 * FD), F32),
         in_specs=[hbm, hbm, hbm, hbm, smem, smem, hbm],
-        out_specs=(vmem, vmem),
+        out_specs=vmem,
         scratch_shapes=[
             pltpu.VMEM((nb, nb), BF16),
             pltpu.VMEM((nb, nb), BF16),
@@ -400,10 +472,13 @@
             pltpu.VMEM((R, nb), F32),
             pltpu.VMEM((16, nb), BF16),
             pltpu.VMEM((32, nb), BF16),
+            pltpu.VMEM((16, nb), BF16),
+            pltpu.VMEM((32, nb), BF16),
+            pltpu.VMEM((8, 8, LANES), F32),
             pltpu.VMEM((8 * gx_n, 8 * gy_n), BF16),
-            pltpu.VMEM((3, gy_n, 8, LANES), F32),
-            pltpu.VMEM((2, gx_n, 8, LANES), F32),
-            pltpu.VMEM((3, gx_n, 8, LANES), F32),
+            pltpu.VMEM((3, gy_n, 4, LANES), F32),
+            pltpu.VMEM((2, gx_n, 4, LANES), F32),
+            pltpu.VMEM((3, gx_n, 4, LANES), F32),
             pltpu.SemaphoreType.DMA((5,)),
             pltpu.SemaphoreType.DMA((2, 3)),
             pltpu.SemaphoreType.DMA((2, 3)),
@@ -416,6 +491,14 @@
             collective_id=0, has_side_effects=True, vmem_limit_bytes=56 * 1024 * 1024
         ),
     )(forcing_terms, schur, flexibility, coarse_modes, coarse_map, face_slot_count, coarse_inverse)
+    out = jax.ShapeDtypeStruct(forcing_terms.shape, F32)
+    return pl.pallas_call(
+        hand_out,
+        out_shape=(out, out),
+        in_specs=[vmem],
+        out_specs=(hbm, hbm),
+        scratch_shapes=[pltpu.SemaphoreType.DMA((2,))],
+    )(both)
 
 
 def solution(mesh):

time: 59.7 us -> 54.8 us (0.918)
  Pallas kernels: 55.8 us -> 53.3 us
  local copies, waits for them, and re-layouts: 3.14 us -> 0.69 us
    pallas_call x1 -> x2, Pallas kernels: 55.8 us -> 53.3 us  [the longest x1 51.6 us: on_device(): pl.pallas_call(functools.partial(kernel, gx_n, gy_n), out_shape=pltpu.VME...]
    unnamed x2, local copies, waits for them, and re-layouts: 3.14 us -> 0.69 us
where the time goes in v3:
time: 54.8 us; the launch traced here: 54.6 us
  Pallas kernels  53.3 us (97%)
  local copies, waits for them, and re-layouts  0.69 us (1%)
  between operations  0.65 us (1%)
    pallas_call x1, Pallas kernels, on_device(): pl.pallas_call(functools.partial(kernel, gx_n, gy_n), out_shape=pltpu.VME...  51.6 us
    pallas_call x1, Pallas kernels, on_device(): pl.pallas_call(hand_out, out_shape=(out, out), in_specs=[vmem], out_specs...  1.66 us

profile of v3, /device:TPU:1, one launch (start us, length us, event | category | flops | bytes accessed | tf_op | source)
XLA Modules:
  0.0 54.6 jit_solution(8526848456600253367)
XLA Ops:
  0.6 51.6 %shard_map.86.both = f32[2,64,512]{2,1,0:T(8,128)S(1)} custom-call(f32[1,1,64,512]{3,2,1,0:T(8,128)} %f_hbm.1, bf16[1,1,1024,1024]{3,2,1,0:T(8,128)(2,1)} %s_hbm.1, bf16[1,1,1024,1024]{3,2,1,0:T(8,128)(2,1)} %a_hbm.1, f32[1,1,8,512]{3,2,1,0:T(8,128)} %modes_hbm.1, s32[1,1,8]{2,1,0:T(1,128)} %map_smem.1, s32[1,1,2]{2,1,0:T(1,128)} %cnt_smem.1, ...), custom_call_target="tpu_custom_call" | custom-call | tf_op jit(solution)/shard_map/pallas_call | solution.py:453
  52.2 0.0 copy-start
  52.3 0.7 %copy-done = f32[2,64,512]{2,1,0:T(8,128)} copy-done((f32[2,64,512]{2,1,0:T(8,128)}, f32[2,64,512]{2,1,0:T(8,128)S(1)}, u32[]{:S(2)}) %copy-start) | copy-done | bytes 262168
  52.9 1.7 %shard_map.87 = (f32[1,1,64,512]{3,2,1,0:T(8,128)}, f32[1,1,64,512]{3,2,1,0:T(8,128)}) custom-call(f32[2,64,512]{2,1,0:T(8,128)} %copy-done), custom_call_target="tpu_custom_call" | custom-call | tf_op jit(solution)/shard_map/pallas_call | solution.py:495
Async XLA Ops:
  52.2 0.7 %copy-start = (f32[2,64,512]{2,1,0:T(8,128)}, f32[2,64,512]{2,1,0:T(8,128)S(1)}, u32[]{:S(2)}) copy-start(f32[2,64,512]{2,1,0:T(8,128)S(1)} %shard_map.86.both) | copy-start | bytes 786436

commit v4 on v3

--- a/solution.py
+++ b/solution.py
@@ -34,10 +34,10 @@
     f_hbm, s_hbm, a_hbm, modes_hbm, map_smem, cnt_smem, cinv_hbm,
     out_v,
     s_v, a_v, cinv_v, f_v, modes_v,
-    stat_v, hf_v, hm_v, hs_v,
-    wsend, wrecv, xz_v, xq_v, xu_v, oe_v, oe2_v, oef_v, oef2_v, gram_v, q_v,
+    stat_v, fs_v, hf_v, hm_v, hs_v,
+    wsend, wrecv, wlast, wshort, xz_v, xq_v, xu_v, oe_v, oe2_v, oef_v, oef2_v, gram_v, q_v,
     g1_v, part_v, g2_v,
-    lsem, hsend, hrecv, wssem, wrsem, gssem, grsem,
+    lsem, hsend, hrecv, wssem, wrsem, gssem, grsem, met_sem,
 ):
     sx = lax.axis_index("gx")
     cy = lax.axis_index("gy")
@@ -68,10 +68,26 @@
 
         lax.fori_loop(1, half, pair, 0)
 
+    x_n, z_n = 4, gx_n // 4
+    x_at, z_at = sx // z_n, lax.rem(sx, z_n)
+
+    def each_z(send):
+        half = z_n // 2
+        send(x_at * z_n + lax.rem(z_at + half, z_n))
+
+        def pair(i, carry):
+            send(x_at * z_n + lax.rem(z_at + half + i, z_n))
+            send(x_at * z_n + lax.rem(z_at + half - i, z_n))
+            return carry
+
+        lax.fori_loop(1, half, pair, 0)
+
+    def each_x(send):
+        for dx in (2, 1, 3):
+            send(lax.rem(x_at + dx, x_n) * z_n + z_at)
+
     def each_column(send):
-        x_n, z_n = 4, gx_n // 4
         half = z_n // 2
-        x_at, z_at = sx // z_n, lax.rem(sx, z_n)
 
         def level(dz, shifts=(2, 1, 3, 0)):
             z_to = lax.rem(z_at + dz, z_n)
@@ -93,8 +109,11 @@
     def greet(target):
         pl.semaphore_signal(barrier, inc=1, device_id=target, device_id_type=MESH)
 
-    each_column(lambda to: greet((to, cy)))
+    each_z(lambda to: greet((to, cy)))
     each_row(lambda to: greet((sx, to)))
+    each_x(lambda to: greet((to, cy)))
+    greet((up_x, cy))
+    greet((dn_x, cy))
 
     lane = lax.broadcasted_iota(jnp.int32, (8, FD), 1)
     sub = lax.broadcasted_iota(jnp.int32, (8, FD), 0)
@@ -223,26 +242,32 @@
 
     def face_copy(op, block):
         return pltpu.make_async_remote_copy(
-            src_ref=wsend.at[op, block], dst_ref=wrecv.at[op, block ^ 1],
+            src_ref=wshort.at[op, block] if op < 3 else wsend.at[op, block],
+            dst_ref=wrecv.at[op, block ^ 1] if op < 3 else wlast.at[block ^ 1],
             send_sem=wssem.at[op, block], recv_sem=wrsem.at[op, block ^ 1],
             device_id=targets[block], device_id_type=MESH,
         )
+
+    def send_face(op, block):
+        if op < 3:
+            wshort[op, block] = wsend[op, block].astype(BF16)
+        face_copy(op, block).start()
 
     def apply(op, xx, matrix, send=True):
         for block in range(4):
             out = jnp.dot(xx, matrix[:, block * FD : (block + 1) * FD], preferred_element_type=F32)
             wsend[op, block] = out[:R] + out[R:]
             if send:
-                face_copy(op, block).start()
+                send_face(op, block)
 
     def add_coarse(op, terms, order, send):
         for block in order:
             wsend[op, block] += coarse_block(terms, oef2_v, block)
             if block in send:
-                face_copy(op, block).start()
+                send_face(op, block)
 
     def collected(op, block):
-        return jnp.where(all_live(block) > 0.5, wsend[op, block] - wrecv[op, block], 0.0)
+        return jnp.where(all_live(block) > 0.5, wsend[op, block] - (wrecv[op, block].astype(F32) if op < 3 else wlast[block]), 0.0)
 
     def wait_faces(op, blocks=(0, 1, 2, 3)):
         for block in blocks:
@@ -255,20 +280,22 @@
         cols = slice(face * FD, (face + 1) * FD)
         live = own_live(face)
         r_own.append(jnp.where(live > 0.5, f_v[:, cols], 0.0))
+        fs_v[face] = r_own[face].astype(BF16)
         basis_block(2 * face + 1, stat_v[face, 0:8, :], modes_v[:, cols] * live)
     basis_own = jnp.concatenate([oe_v[:, FD : 2 * FD], oe_v[:, 3 * FD :]], axis=1)
     first_sums = restrict(split_rows(jnp.concatenate(r_own, axis=1)), basis_own)
 
-    pl.semaphore_wait(barrier, gy_n + gx_n - 2)
+    pl.semaphore_wait(barrier, gy_n + z_n + x_n - 1)
 
     row_send(0, first_sums)
+    each_x(lambda to: pl.semaphore_signal(met_sem, inc=1, device_id=(to, cy), device_id_type=MESH))
     halo = []
     for face, target in ((0, (up_x, cy)), (1, (sx, up_y))):
         cols = pl.ds(face * FD, FD)
         for n, (src, dst) in enumerate((
             (stat_v.at[face], hs_v.at[face]),
             (modes_v.at[:, cols], hm_v.at[face]),
-            (f_v.at[:, cols], hf_v.at[face]),
+            (fs_v.at[face], hf_v.at[face]),
         )):
             copy = pltpu.make_async_remote_copy(
                 src_ref=src, dst_ref=dst, send_sem=hsend.at[face, n], recv_sem=hrecv.at[face, n],
@@ -303,15 +330,16 @@
     halo[3].wait_recv()
     x0 = jnp.concatenate(
         [
-            -jnp.where(all_live(0) > 0.5, hf_v[0], 0.0),
+            -jnp.where(all_live(0) > 0.5, hf_v[0].astype(F32), 0.0),
             r_own[0],
-            -jnp.where(all_live(2) > 0.5, hf_v[1], 0.0),
+            -jnp.where(all_live(2) > 0.5, hf_v[1].astype(F32), 0.0),
             r_own[1],
         ],
         axis=1,
     )
     loads[3].wait()
     apply(0, split_rows(x0), s_v)
+    pl.semaphore_wait(met_sem, x_n - 1)
     solve(0)
 
     halo[1].wait_recv()
@@ -462,11 +490,14 @@
             pltpu.VMEM((R, 2 * FD), F32),
             pltpu.VMEM((8, 2 * FD), F32),
             pltpu.VMEM((2, 16, FD), F32),
-            pltpu.VMEM((2, R, FD), F32),
+            pltpu.VMEM((2, R, FD), BF16),
+            pltpu.VMEM((2, R, FD), BF16),
             pltpu.VMEM((2, 8, FD), F32),
             pltpu.VMEM((2, 16, FD), F32),
             pltpu.VMEM((4, 4, R, FD), F32),
-            pltpu.VMEM((4, 4, R, FD), F32),
+            pltpu.VMEM((3, 4, R, FD), BF16),
+            pltpu.VMEM((4, R, FD), F32),
+            pltpu.VMEM((3, 4, R, FD), BF16),
             pltpu.VMEM((R, nb), F32),
             pltpu.VMEM((R, nb), F32),
             pltpu.VMEM((R, nb), F32),
@@ -486,6 +517,7 @@
             pltpu.SemaphoreType.DMA((4, 4)),
             pltpu.SemaphoreType.DMA((3, 2)),
             pltpu.SemaphoreType.DMA((3, 2)),
+            pltpu.SemaphoreType.REGULAR,
         ],
         compiler_params=pltpu.CompilerParams(
             collective_id=0, has_side_effects=True, vmem_limit_bytes=56 * 1024 * 1024
@@ -498,7 +530,7 @@
         in_specs=[vmem],
         out_specs=(hbm, hbm),
         scratch_shapes=[pltpu.SemaphoreType.DMA((2,))],
-    )(both)
+    )(pltpu.with_memory_space_constraint(both, pltpu.VMEM))
 
 
 def solution(mesh):

time: 54.8 us -> 51 us (0.931)
  Pallas kernels: 53.3 us -> 50.2 us
  local copies, waits for them, and re-layouts: 0.69 us -> 0 us
    pallas_call x1, Pallas kernels: 51.6 us -> 49.5 us  [on_device(): pl.pallas_call(functools.partial(kernel, gx_n, gy_n), out_shape=pltpu.VME...]
    pallas_call x1, Pallas kernels: 1.66 us -> 0.72 us  [on_device(): pl.pallas_call(hand_out, out_shape=(out, out), in_specs=[vmem], out_specs...]
    unnamed x2 -> x0, local copies, waits for them, and re-layouts: 0.69 us -> none
where the time goes in v4:
time: 51 us; the launch traced here: 50.9 us
  Pallas kernels  50.2 us (98%)
  between operations  0.64 us (1%)
    pallas_call x1, Pallas kernels, on_device(): pl.pallas_call(functools.partial(kernel, gx_n, gy_n), out_shape=pltpu.VME...  49.5 us

profile of v4, /device:TPU:1, one launch (start us, length us, event | category | flops | bytes accessed | tf_op | source)
XLA Modules:
  0.0 50.9 jit_solution(7590913293534169753)
XLA Ops:
  0.6 49.5 %shard_map.86.both = f32[2,64,512]{2,1,0:T(8,128)S(1)} custom-call(f32[1,1,64,512]{3,2,1,0:T(8,128)} %f_hbm.1, bf16[1,1,1024,1024]{3,2,1,0:T(8,128)(2,1)} %s_hbm.1, bf16[1,1,1024,1024]{3,2,1,0:T(8,128)(2,1)} %a_hbm.1, f32[1,1,8,512]{3,2,1,0:T(8,128)} %modes_hbm.1, s32[1,1,8]{2,1,0:T(1,128)} %map_smem.1, s32[1,1,2]{2,1,0:T(1,128)} %cnt_smem.1, ...), custom_call_target="tpu_custom_call" | custom-call | tf_op jit(solution)/shard_map/pallas_call | solution.py:481
  50.1 0.7 %shard_map.87 = (f32[1,1,64,512]{3,2,1,0:T(8,128)}, f32[1,1,64,512]{3,2,1,0:T(8,128)}) custom-call(f32[2,64,512]{2,1,0:T(8,128)S(1)} %shard_map.86.both), custom_call_target="tpu_custom_call" | custom-call | tf_op jit(solution)/shard_map/pallas_call | solution.py:527
